TPU v7x, 128 devices: a whole 4x4x4 slice. The times are simulated.
128 devices in a mesh: ctx: 8 (over y, core), head: 16 (over x, z).
Axes of the slice: x: 4, y: 4, z: 4, core: 2. Of those that a mesh axis runs over, the one named last changes fastest.
Arguments:
- ssm_input: bfloat16 [16384, 16384], P('ctx', 'head'), may hold values from -6 to 6
- step_size: float32 [16384, 256], P('ctx', 'head'), may hold values from 0.0625 to 16
- decay_rate: float32 [256], P('head'), may hold values from 2e-05 to 0.04
- skip_gain: float32 [256], P('head'), may hold values from 0.5 to 1.5
- input_proj: bfloat16 [16384, 8, 256], P('ctx'), may hold values from -0.375 to 0.375
- output_proj: bfloat16 [16384, 8, 256], P('ctx'), may hold values from -0.375 to 0.375
- out_grad: bfloat16 [16384, 16384], P(('ctx', 'head')), may hold values from -3 to 3
Outputs:
- input_grad: bfloat16 [16384, 16384], P(('ctx', 'head'))
- step_grad: float32 [16384, 256], P('ctx', 'head')
All inputs are finite; a program needn't handle non-finite values.
Results may differ from a plain program's by a relative error of at most 0.001.
Values may be sent and summed in bfloat16 or wider, within the bound.
A program may use at most 256 MiB of HBM per device.

v0:
```python
import jax
import jax.numpy as jnp
from jax import lax
from jax.experimental import pallas as pl
from jax.experimental.pallas import tpu as pltpu
from jax.sharding import PartitionSpec as P

NHEAD = 16
NY = 4
LOCAL = 2048
ROWS = 128
COLS = 1024
BLK = 256
NBLK = LOCAL // BLK
GC = 256
NG = COLS // GC
NGROUPS = 8
CH = 128
NCH = LOCAL // CH
MESH = pl.DeviceIdType.MESH
F32 = jnp.float32
BF16 = jnp.bfloat16


def mm(a, b):
    return jnp.dot(a, b, preferred_element_type=F32)


def exact_mm(a, b):
    return jnp.dot(a, b, preferred_element_type=F32, precision=lax.Precision.HIGHEST)


def halves(v):
    hi = v.astype(BF16)
    return hi, (v - hi.astype(F32)).astype(BF16)


def iota(shape, dim):
    return lax.broadcasted_iota(jnp.int32, shape, dim)


def pack3(v):
    hi = v.astype(BF16).astype(F32)
    rest = v - hi
    md = rest.astype(BF16).astype(F32)
    parts = jnp.concatenate([hi, md, rest - md, jnp.zeros((80, v.shape[1]), F32)], axis=0)
    return parts.T.astype(BF16)


def kernel(
    x_hbm, step_ref, rate_ref, gain_ref, b_hbm, c_hbm, g_hbm, out_hbm, sg_ref,
    xo, gv, xh, xl, agh, agl, tf, ta, raw, bm, cm, bt, ct, cbh, cbl, bch, bcl,
    asp, bsp, expand, acc, res, qe, we, de, lbuf,
    fs_tot, fs_pair, fs_chip, fs_in, as_tot, as_pair, as_chip, as_in,
    loc_sem, raw_sem, gs, gr, os, orr, ls, lr, fps, fpr, fys, fyr, aps, apr, ays, ayr,
):
    c = lax.axis_index("ctx")
    h = lax.axis_index("head")
    hx, hz = h // 4, lax.rem(h, 4)
    y, k = c // 2, lax.rem(c, 2)
    group = h // 2
    core0 = k == 0

    def head_at(j):
        return lax.rem(hx + j // 4, 4) * 4 + lax.rem(hz + lax.rem(j, 4), 4)

    def head_from(j):
        return lax.rem(hx + 4 - j // 4, 4) * 4 + lax.rem(hz + 4 - lax.rem(j, 4), 4)

    def cols(grp):
        return pl.ds(grp * GC, GC)

    x_copy = pltpu.make_async_copy(x_hbm, xo, loc_sem.at[0])
    x_copy.start()

    def raw_copies(i):
        rows = pl.ds(pl.multiple_of(i * (CH * NGROUPS), CH * NGROUPS), CH * NGROUPS)
        slot = lax.rem(i, 2)
        return (
            pltpu.make_async_copy(b_hbm.at[rows], raw.at[slot, 0], raw_sem.at[slot, 0]),
            pltpu.make_async_copy(c_hbm.at[rows], raw.at[slot, 1], raw_sem.at[slot, 1]),
        )

    for cp in raw_copies(0):
        cp.start()

    barrier = pltpu.get_barrier_semaphore()

    @pl.loop(1, NHEAD)
    def _(j):
        pl.semaphore_signal(barrier, 1, device_id=(c, head_at(j)), device_id_type=MESH)

    @pl.loop(1, 8)
    def _(j):
        pl.semaphore_signal(barrier, 1, device_id=(lax.rem(c + j, 8), h), device_id_type=MESH)

    pl.semaphore_wait(barrier, NHEAD - 1 + 7)

    def grad_in(grp, j):
        to = head_at(j)
        return pltpu.make_async_remote_copy(
            g_hbm.at[:, pl.ds(pl.multiple_of(to * COLS + grp * GC, GC), GC)],
            gv.at[pl.ds(pl.multiple_of(h * ROWS, ROWS), ROWS), cols(grp)],
            gs.at[grp, j],
            gr.at[grp, j],
            device_id=(c, to),
            device_id_type=MESH,
        )

    for grp in range(NG):

        @pl.loop(1, NHEAD)
        def _(j):
            grad_in(grp, j).start()

    own_g = pltpu.make_async_copy(
        g_hbm.at[:, pl.ds(pl.multiple_of(h * COLS, COLS), COLS)],
        gv.at[pl.ds(pl.multiple_of(h * ROWS, ROWS), ROWS)],
        loc_sem.at[1],
    )
    own_g.start()

    eye16 = iota((16, 16), 0) == iota((16, 16), 1)
    rate = jnp.sum(jnp.where(eye16, rate_ref[...], 0.0), axis=1, keepdims=True)
    gain = jnp.sum(jnp.where(eye16, gain_ref[...], 0.0), axis=1, keepdims=True)
    kk = iota((128, COLS), 0)
    expand[...] = jnp.where(
        (kk < 48) & (lax.rem(kk, 16) == iota((128, COLS), 1) // 64), 1.0, 0.0
    ).astype(BF16)
    before = (iota((BLK, BLK), 0) <= iota((BLK, BLK), 1)).astype(F32)
    lane = iota((16, 128), 1)
    mids = jnp.zeros((16, 128), F32)
    log_own = jnp.zeros((16, 1), F32)
    for blk in range(NBLK):
        st = step_ref[:, blk * BLK : (blk + 1) * BLK]
        cum = exact_mm(-rate * st, before)
        total = cum[:, BLK - 1 : BLK]
        mid = 0.5 * total
        mids = jnp.where(lane == blk, mid, mids)
        log_own = log_own + total
        asp[blk] = pack3(jnp.exp(cum - mid))
        bsp[blk] = pack3(st * jnp.exp(mid - cum) * 0.0625)
    qe[...] = mm(pack3(jnp.where(lane == 8, gain, jnp.exp(mids)))[:16], expand[...])
    lbuf[c] = jnp.broadcast_to(log_own, (16, 128))

    def log_send(j):
        return pltpu.make_async_remote_copy(
            lbuf.at[c], lbuf.at[c], ls.at[j], lr.at[j],
            device_id=(lax.rem(c + j, 8), h), device_id_type=MESH,
        )

    @pl.loop(1, 8)
    def _(j):
        log_send(j).start()

    pick = jnp.where(iota((32, 256), 1) == iota((32, 256), 0) * NGROUPS + group, 1.0, 0.0)
    pick = pick.astype(BF16)

    @pl.loop(0, NCH)
    def _(i):
        @pl.when(i + 1 < NCH)
        def _():
            for cp in raw_copies(i + 1):
                cp.start()

        for cp in raw_copies(i):
            cp.wait()
        slot = lax.rem(i, 2)
        at = pl.multiple_of(i * CH, CH)
        for which, target in ((0, bm), (1, cm)):
            for part in range(CH // 32):
                rows = raw[slot, which, pl.ds(part * 256, 256), :]
                target[pl.ds(at + part * 32, 32), :] = mm(pick, rows).astype(BF16)

    low = iota((BLK, BLK), 0) >= iota((BLK, BLK), 1)

    @pl.loop(0, NBLK)
    def _(blk):
        at = pl.ds(pl.multiple_of(blk * BLK, BLK), BLK)
        b, cc = bm[at, :], cm[at, :]
        btr, ctr = b.T, cc.T
        bt[at, :] = btr
        ct[at, :] = ctr
        cbh[at, :], cbl[at, :] = halves(jnp.where(low, mm(cc, btr), 0.0))
        bch[at, :], bcl[at, :] = halves(jnp.where(low, mm(cc, btr), 0.0).T)

    def pair_copy(src, dst, s, r, grp):
        return pltpu.make_async_remote_copy(
            src.at[grp], dst.at[grp], s.at[grp], r.at[grp],
            device_id=(y * 2 + 1 - k, h), device_id_type=MESH,
        )

    def line_copy(src, dst, s, r, grp, dy, forward):
        to = y + dy if forward else y + 4 - dy
        return pltpu.make_async_remote_copy(
            src.at[grp], dst.at[dy - 1, grp], s.at[dy - 1, grp], r.at[dy - 1, grp],
            device_id=(lax.rem(to, 4) * 2 + k, h), device_id_type=MESH,
        )

    def q_row(blk, grp):
        return qe[pl.ds(blk, 1), cols(grp)]

    def forward_local(grp):
        acc[...] = jnp.zeros_like(acc)

        @pl.loop(0, NBLK)
        def _(blk):
            at = pl.ds(pl.multiple_of(blk * BLK, BLK), BLK)
            xb = xo[at, cols(grp)].astype(F32) * mm(bsp[blk], expand[:, cols(grp)])
            hi, lo = halves(xb)
            xh[at, cols(grp)] = hi
            xl[at, cols(grp)] = lo
            t = mm(bt[at, :], hi) + mm(bt[at, :], lo)
            tf[grp, blk] = t
            q = q_row(blk, grp)
            acc[...] = q * (q * acc[...] + t)

        fs_tot[grp] = acc[...]
        pair_copy(fs_tot, fs_pair, fps, fpr, grp).start()

    def forward_chip(grp):
        pair_copy(fs_tot, fs_pair, fps, fpr, grp).wait()
        fs_chip[grp] = (
            we[0:1, cols(grp)] * fs_tot[grp] + we[1:2, cols(grp)] * fs_pair[grp]
        ).astype(BF16)
        for dy in (1, 2, 3):

            @pl.when(y + dy < NY)
            def _():
                line_copy(fs_chip, fs_in, fys, fyr, grp, dy, True).start()

    def forward_states(grp):
        acc[...] = jnp.zeros_like(acc)
        for dy in (1, 2, 3):

            @pl.when(y - dy >= 0)
            def _():
                line_copy(fs_chip, fs_in, fys, fyr, grp, dy, True).wait_recv()
                acc[...] += we[2 + dy : 3 + dy, cols(grp)] * fs_in[dy - 1, grp].astype(F32)

        acc[...] = we[2:3, cols(grp)] * acc[...]

        @pl.when(k == 1)
        def _():
            acc[...] += fs_pair[grp]

        @pl.loop(0, NBLK)
        def _(blk):
            q = q_row(blk, grp)
            scaled = q * acc[...]
            acc[...] = q * (scaled + tf[grp, blk])
            tf[grp, blk] = scaled

        fs_tot[grp] = acc[...]

    def adjoint_local(grp):
        slot = grp % 2

        @pl.loop(1, NHEAD)
        def _(j):
            grad_in(grp, j).wait_recv()

        acc[...] = jnp.zeros_like(acc)

        @pl.loop(0, NBLK)
        def _(i):
            blk = NBLK - 1 - i
            at = pl.ds(pl.multiple_of(blk * BLK, BLK), BLK)
            ag = gv[at, cols(grp)].astype(F32) * mm(asp[blk], expand[:, cols(grp)])
            hi, lo = halves(ag)
            agh[slot, at, :] = hi
            agl[slot, at, :] = lo
            t = mm(ct[at, :], hi) + mm(ct[at, :], lo)
            ta[slot, blk] = t
            q = q_row(blk, grp)
            acc[...] = q * (q * acc[...] + t)

        as_tot[grp] = acc[...]
        pair_copy(as_tot, as_pair, aps, apr, grp).start()

    def adjoint_chip(grp):
        pair_copy(as_tot, as_pair, aps, apr, grp).wait()
        as_chip[grp] = we[6:7, cols(grp)] * as_tot[grp] + we[7:8, cols(grp)] * as_pair[grp]
        for dy in (1, 2, 3):

            @pl.when(y - dy >= 0)
            def _():
                line_copy(as_chip, as_in, ays, ayr, grp, dy, False).start()

    def grad_out(grp, j):
        to = head_at(j)
        return pltpu.make_async_remote_copy(
            xo.at[pl.ds(pl.multiple_of(to * ROWS, ROWS), ROWS), cols(grp)],
            out_hbm.at[:, pl.ds(pl.multiple_of(h * COLS + grp * GC, GC), GC)],
            os.at[grp, j],
            orr.at[grp, j],
            device_id=(c, to),
            device_id_type=MESH,
        )

    def own_out(grp):
        return pltpu.make_async_copy(
            xo.at[pl.ds(pl.multiple_of(h * ROWS, ROWS), ROWS), cols(grp)],
            out_hbm.at[:, pl.ds(pl.multiple_of(h * COLS + grp * GC, GC), GC)],
            loc_sem.at[2 + grp],
        )

    def finish(grp):
        slot = grp % 2
        acc[...] = jnp.zeros_like(acc)
        for dy in (1, 2, 3):

            @pl.when(y + dy < NY)
            def _():
                line_copy(as_chip, as_in, ays, ayr, grp, dy, False).wait_recv()
                acc[...] += we[8 + dy : 9 + dy, cols(grp)] * as_in[dy - 1, grp]

        acc[...] = we[8:9, cols(grp)] * acc[...]

        @pl.when(core0)
        def _():
            acc[...] += as_pair[grp]

        de[:, cols(grp)] = jnp.broadcast_to(
            jnp.sum(fs_tot[grp] * acc[...], axis=0, keepdims=True), (8, GC)
        )
        gain_row = qe[8:9, cols(grp)]
        head_of = grp * (GC // 64) + iota((GC, 128), 0) // 64
        to_dc = jnp.where(iota((GC, 128), 1) == head_of, 1.0, 0.0).astype(BF16)
        to_sx = jnp.where(iota((GC, 128), 1) == head_of + 64, 1.0, 0.0).astype(BF16)

        @pl.loop(0, NBLK)
        def _(i):
            blk = NBLK - 1 - i
            at = pl.ds(pl.multiple_of(blk * BLK, BLK), BLK)
            q = q_row(blk, grp)
            scaled = q * acc[...]
            acc[...] = q * (scaled + ta[slot, blk])
            sh, sl = halves(scaled)
            ah, al = agh[slot, at, :], agl[slot, at, :]
            b = bm[at, :]
            gb = mm(bch[at, :], ah) + mm(bcl[at, :], ah) + mm(bch[at, :], al)
            gb = gb + mm(b, sh) + mm(b, sl)
            bs = mm(bsp[blk], expand[:, cols(grp)])
            grads = (16.0 * bs) * gb + gain_row * gv[at, cols(grp)].astype(F32)
            xo[at, cols(grp)] = grads.astype(BF16)
            hi, lo = xh[at, cols(grp)], xl[at, cols(grp)]
            sh, sl = halves(tf[grp, blk])
            cc = cm[at, :]
            yy = mm(cbh[at, :], hi) + mm(cbl[at, :], hi) + mm(cbh[at, :], lo)
            yy = yy + mm(cc, sh) + mm(cc, sl)
            sx = (hi.astype(F32) + lo.astype(F32)) * gb
            dc = (ah.astype(F32) + al.astype(F32)) * yy - sx
            dh, dl = halves(dc)
            xh_, xl_ = halves(sx)
            r = mm(dh, to_dc) + mm(dl, to_dc) + mm(xh_, to_sx) + mm(xl_, to_sx)
            if grp == 0:
                res[blk] = r
            else:
                res[blk] += r

        @pl.loop(1, NHEAD)
        def _(j):
            grad_out(grp, j).start()

        own_out(grp).start()

    x_copy.wait()
    for grp in range(NG):
        forward_local(grp)

    @pl.loop(1, 8)
    def _(j):
        log_send(j).wait()

    def log_chip(at):
        at = lax.rem(at + 8, 4)
        return lbuf[at * 2] + lbuf[at * 2 + 1]

    def put(logs, i, v):
        return jnp.where(lane == i, v, logs)

    mine, other = lbuf[c], lbuf[y * 2 + 1 - k]
    logs = jnp.zeros((16, 128), F32)
    logs = put(logs, 0, jnp.where(core0, other, 0.0))
    logs = put(logs, 1, jnp.where(core0, 0.0, mine))
    logs = put(logs, 2, jnp.where(core0, 0.0, other))
    logs = put(logs, 4, log_chip(y - 1))
    logs = put(logs, 5, log_chip(y - 1) + log_chip(y - 2))
    logs = put(logs, 6, jnp.where(core0, 0.0, other))
    logs = put(logs, 7, jnp.where(core0, mine, 0.0))
    logs = put(logs, 8, jnp.where(core0, other, 0.0))
    logs = put(logs, 10, log_chip(y + 1))
    logs = put(logs, 11, log_chip(y + 1) + log_chip(y + 2))
    we[...] = mm(pack3(jnp.exp(logs))[:16], expand[...])
    own_g.wait()

    for grp in range(NG):
        forward_chip(grp)
    adjoint_local(0)
    adjoint_chip(0)
    forward_states(0)
    adjoint_local(1)
    adjoint_chip(1)
    forward_states(1)
    finish(0)
    adjoint_local(2)
    adjoint_chip(2)
    forward_states(2)
    finish(1)
    adjoint_local(3)
    adjoint_chip(3)
    forward_states(3)
    finish(2)
    finish(3)

    head_of = iota((COLS, 128), 0) // 64
    to_dc = jnp.where(iota((COLS, 128), 1) == head_of, 1.0, 0.0).astype(F32)
    tail = exact_mm(de[...], to_dc)
    tail = jnp.broadcast_to(tail[0:1, :], (128, 128)).T[0:16, 0:1]
    after = (iota((BLK, BLK), 0) >= iota((BLK, BLK), 1)).astype(F32)
    for blk in range(NBLK - 1, -1, -1):
        r = res[blk].T
        suffix = exact_mm(r[0:16], after) + tail
        tail = suffix[:, 0:1]
        at = slice(blk * BLK, (blk + 1) * BLK)
        sg_ref[:, at] = 16.0 * (r[64:80] / step_ref[:, at] - rate * suffix)

    for grp in range(NG):

        @pl.loop(1, NHEAD)
        def _(j):
            grad_in(grp, j).wait_send()
            grad_out(grp, j).wait()

        own_out(grp).wait()
        for dy in (1, 2, 3):

            @pl.when(y + dy < NY)
            def _():
                line_copy(fs_chip, fs_in, fys, fyr, grp, dy, True).wait_send()

            @pl.when(y - dy >= 0)
            def _():
                line_copy(as_chip, as_in, ays, ayr, grp, dy, False).wait_send()


def local(ssm_input, step_size, decay_rate, skip_gain, input_proj, output_proj, out_grad):
    vm = pltpu.VMEM
    dma = pltpu.SemaphoreType.DMA
    state = (NG, BLK, GC)
    proj = vm((LOCAL, BLK), BF16)
    scratch = [
        vm((LOCAL, COLS), BF16),
        vm((LOCAL, COLS), BF16),
        vm((LOCAL, COLS), BF16),
        vm((LOCAL, COLS), BF16),
        vm((2, LOCAL, GC), BF16),
        vm((2, LOCAL, GC), BF16),
        vm((NG, NBLK, BLK, GC), F32),
        vm((2, NBLK, BLK, GC), F32),
        vm((2, 2, CH * NGROUPS, BLK), BF16),
    ]
    scratch += [proj] * 8
    scratch += [
        vm((NBLK, BLK, 128), BF16),
        vm((NBLK, BLK, 128), BF16),
        vm((128, COLS), BF16),
        vm((BLK, GC), F32),
        vm((NBLK, BLK, 128), F32),
        vm((16, COLS), F32),
        vm((16, COLS), F32),
        vm((8, COLS), F32),
        vm((8, 16, 128), F32),
        vm(state, F32),
        vm(state, F32),
        vm(state, BF16),
        vm((3,) + state, BF16),
        vm(state, F32),
        vm(state, F32),
        vm(state, F32),
        vm((3,) + state, F32),
        dma((2 + NG,)),
        dma((2, 2)),
        dma((NG, NHEAD)), dma((NG, NHEAD)), dma((NG, NHEAD)), dma((NG, NHEAD)),
        dma((8,)), dma((8,)),
        dma((NG,)), dma((NG,)), dma((3, NG)), dma((3, NG)),
        dma((NG,)), dma((NG,)), dma((3, NG)), dma((3, NG)),
    ]
    hbm = pl.BlockSpec(memory_space=pl.ANY)
    vmem = pl.BlockSpec(memory_space=pltpu.VMEM)
    grads, steps = pl.pallas_call(
        kernel,
        out_shape=(
            jax.ShapeDtypeStruct((ROWS, NHEAD * COLS), BF16),
            jax.ShapeDtypeStruct((16, LOCAL), F32),
        ),
        in_specs=[hbm, vmem, vmem, vmem, hbm, hbm, hbm],
        out_specs=(hbm, vmem),
        scratch_shapes=scratch,
        compiler_params=pltpu.CompilerParams(
            collective_id=0, has_side_effects=True, vmem_limit_bytes=62 << 20
        ),
    )(
        ssm_input,
        step_size.T,
        decay_rate.reshape(1, 16),
        skip_gain.reshape(1, 16),
        input_proj.reshape(LOCAL * NGROUPS, BLK),
        output_proj.reshape(LOCAL * NGROUPS, BLK),
        out_grad,
    )
    return grads, steps.T


def solution(mesh):
    in_specs = (
        P("ctx", "head"),
        P("ctx", "head"),
        P("head"),
        P("head"),
        P("ctx", None, None),
        P("ctx", None, None),
        P(("ctx", "head"), None),
    )
    out_specs = (P(("ctx", "head"), None), P("ctx", "head"))
    return jax.shard_map(local, mesh=mesh, in_specs=in_specs, out_specs=out_specs, check_vma=False)
```

profile of v0, /device:TPU:4, one launch (start us, length us, event | category | flops | bytes accessed | tf_op | source)
XLA Modules:
  0.0 136.4 jit_solution(15675342148094776591)
XLA Ops:
  0.6 130.5 %shard_map.86 = (bf16[128,16384]{1,0:T(8,128)(2,1)}, f32[16,2048]{1,0:T(8,128)}) custom-call(bf16[2048,1024]{1,0:T(8,128)(2,1)} %x_hbm.1, f32[16,2048]{1,0:T(8,128)} %bitcast.8, f32[1,16]{1,0:T(1,128)} %bitcast.10, f32[1,16]{1,0:T(1,128)} %bitcast.11, bf16[16384,256]{1,0:T(8,128)(2,1)} %bitcast.6, bf16[16384,256]{1,0:T(8,128)(2,1)} %bitcast.7, ...), custom_call_target="tpu_custom_call" | custom-call | tf_op jit(solution)/shard_map/pallas_call | solution.py:492
  131.2 0.0 copy-start
  131.2 4.6 %copy.11 = bf16[128,16384]{1,0:T(8,128)(2,1)} copy(bf16[128,16384]{1,0:T(8,128)(2,1)} %get-tuple-element.8) | data formatting | bytes 8388608
  135.8 0.0 copy-done
  135.8 0.7 copy.12
Async XLA Ops:
  131.2 4.6 %copy-start = (f32[16,2048]{1,0:T(8,128)S(1)}, f32[16,2048]{1,0:T(8,128)}, u32[]{:S(2)}) copy-start(f32[16,2048]{1,0:T(8,128)} %get-tuple-element.5) | copy-start | bytes 393220
where the time goes:
time: 137 us; the launch traced here: 136 us
  Pallas kernels  131 us (96%)
  local copies, waits for them, and re-layouts  5.27 us (4%)
    pallas_call x1, Pallas kernels, local(): pl.pallas_call(kernel, out_shape=(jax.ShapeDtypeStruct((ROWS, NHEAD * COL...  131 us
    unnamed x4, local copies, waits for them, and re-layouts  5.27 us

commit v1 on v0

--- a/solution.py
+++ b/solution.py
@@ -11,10 +11,12 @@
 ROWS = 128
 COLS = 1024
 BLK = 256
+HALF = BLK // 2
 NBLK = LOCAL // BLK
 GC = 256
 NG = COLS // GC
 NGROUPS = 8
+GAIN_ROW = 6 * NBLK
 CH = 128
 NCH = LOCAL // CH
 MESH = pl.DeviceIdType.MESH
@@ -28,6 +30,14 @@
 
 def exact_mm(a, b):
     return jnp.dot(a, b, preferred_element_type=F32, precision=lax.Precision.HIGHEST)
+
+
+def twice(a):
+    return jnp.concatenate([a, a], axis=1)
+
+
+def whole(parts):
+    return parts[:HALF].astype(F32) + parts[HALF:].astype(F32)
 
 
 def halves(v):
@@ -49,7 +59,7 @@
 
 def kernel(
     x_hbm, step_ref, rate_ref, gain_ref, b_hbm, c_hbm, g_hbm, out_hbm, sg_ref,
-    xo, gv, xh, xl, agh, agl, tf, ta, raw, bm, cm, bt, ct, cbh, cbl, bch, bcl,
+    xo, gv, xs, ags, tf, ta, raw, bm, cm, bt, ct, cbh, cbl, bch, bcl,
     asp, bsp, expand, acc, res, qe, we, de, lbuf,
     fs_tot, fs_pair, fs_chip, fs_in, as_tot, as_pair, as_chip, as_in,
     loc_sem, raw_sem, gs, gr, os, orr, ls, lr, fps, fpr, fys, fyr, aps, apr, ays, ayr,
@@ -129,18 +139,21 @@
     ).astype(BF16)
     before = (iota((BLK, BLK), 0) <= iota((BLK, BLK), 1)).astype(F32)
     lane = iota((16, 128), 1)
-    mids = jnp.zeros((16, 128), F32)
+    logs = jnp.zeros((16, 128), F32)
     log_own = jnp.zeros((16, 1), F32)
     for blk in range(NBLK):
         st = step_ref[:, blk * BLK : (blk + 1) * BLK]
         cum = exact_mm(-rate * st, before)
         total = cum[:, BLK - 1 : BLK]
-        mid = 0.5 * total
-        mids = jnp.where(lane == blk, mid, mids)
+        half = cum[:, HALF - 1 : HALF]
+        mid1, mid2 = 0.5 * half, 0.5 * (half + total)
+        for row, v in enumerate((total, total - mid1, total - mid2, mid1, mid2, mid2 - mid1)):
+            logs = jnp.where(lane == row * NBLK + blk, v, logs)
         log_own = log_own + total
+        mid = jnp.where(iota((16, BLK), 1) < HALF, mid1, mid2)
         asp[blk] = pack3(jnp.exp(cum - mid))
-        bsp[blk] = pack3(st * jnp.exp(mid - cum) * 0.0625)
-    qe[...] = mm(pack3(jnp.where(lane == 8, gain, jnp.exp(mids)))[:16], expand[...])
+        bsp[blk] = pack3(st * jnp.exp(mid - cum))
+    qe[...] = mm(pack3(jnp.where(lane == GAIN_ROW, gain, jnp.exp(logs)))[:56], expand[...])
     lbuf[c] = jnp.broadcast_to(log_own, (16, 128))
 
     def log_send(j):
@@ -197,8 +210,8 @@
             device_id=(lax.rem(to, 4) * 2 + k, h), device_id_type=MESH,
         )
 
-    def q_row(blk, grp):
-        return qe[pl.ds(blk, 1), cols(grp)]
+    def scale(which, blk, grp):
+        return qe[pl.ds(which * NBLK + blk, 1), cols(grp)]
 
     def forward_local(grp):
         acc[...] = jnp.zeros_like(acc)
@@ -206,14 +219,16 @@
         @pl.loop(0, NBLK)
         def _(blk):
             at = pl.ds(pl.multiple_of(blk * BLK, BLK), BLK)
-            xb = xo[at, cols(grp)].astype(F32) * mm(bsp[blk], expand[:, cols(grp)])
-            hi, lo = halves(xb)
-            xh[at, cols(grp)] = hi
-            xl[at, cols(grp)] = lo
-            t = mm(bt[at, :], hi) + mm(bt[at, :], lo)
+            t = jnp.zeros((BLK, GC), F32)
+            for i in range(2):
+                here = pl.ds(pl.multiple_of(blk * BLK + i * HALF, HALF), HALF)
+                part = slice(i * HALF, (i + 1) * HALF)
+                bs = mm(bsp[blk, part, :], expand[:, cols(grp)])
+                pair = jnp.concatenate(halves(xo[here, cols(grp)].astype(F32) * bs), axis=0)
+                xs[2 * blk + i, :, cols(grp)] = pair
+                t = t + scale(1 + i, blk, grp) * mm(twice(bt[at, part]), pair)
             tf[grp, blk] = t
-            q = q_row(blk, grp)
-            acc[...] = q * (q * acc[...] + t)
+            acc[...] = scale(0, blk, grp) * acc[...] + t
 
         fs_tot[grp] = acc[...]
         pair_copy(fs_tot, fs_pair, fps, fpr, grp).start()
@@ -246,12 +261,11 @@
 
         @pl.loop(0, NBLK)
         def _(blk):
-            q = q_row(blk, grp)
-            scaled = q * acc[...]
-            acc[...] = q * (scaled + tf[grp, blk])
-            tf[grp, blk] = scaled
-
-        fs_tot[grp] = acc[...]
+            entry = acc[...]
+            acc[...] = scale(0, blk, grp) * entry + tf[grp, blk]
+            tf[grp, blk] = entry
+
+        tf[grp, NBLK] = acc[...]
 
     def adjoint_local(grp):
         slot = grp % 2
@@ -263,17 +277,19 @@
         acc[...] = jnp.zeros_like(acc)
 
         @pl.loop(0, NBLK)
-        def _(i):
-            blk = NBLK - 1 - i
+        def _(lap):
+            blk = NBLK - 1 - lap
             at = pl.ds(pl.multiple_of(blk * BLK, BLK), BLK)
-            ag = gv[at, cols(grp)].astype(F32) * mm(asp[blk], expand[:, cols(grp)])
-            hi, lo = halves(ag)
-            agh[slot, at, :] = hi
-            agl[slot, at, :] = lo
-            t = mm(ct[at, :], hi) + mm(ct[at, :], lo)
+            t = jnp.zeros((BLK, GC), F32)
+            for i in range(2):
+                here = pl.ds(pl.multiple_of(blk * BLK + i * HALF, HALF), HALF)
+                part = slice(i * HALF, (i + 1) * HALF)
+                a = mm(asp[blk, part, :], expand[:, cols(grp)])
+                pair = jnp.concatenate(halves(gv[here, cols(grp)].astype(F32) * a), axis=0)
+                ags[slot, 2 * blk + i] = pair
+                t = t + scale(3 + i, blk, grp) * mm(twice(ct[at, part]), pair)
             ta[slot, blk] = t
-            q = q_row(blk, grp)
-            acc[...] = q * (q * acc[...] + t)
+            acc[...] = scale(0, blk, grp) * acc[...] + t
 
         as_tot[grp] = acc[...]
         pair_copy(as_tot, as_pair, aps, apr, grp).start()
@@ -321,43 +337,56 @@
         def _():
             acc[...] += as_pair[grp]
 
-        de[:, cols(grp)] = jnp.broadcast_to(
-            jnp.sum(fs_tot[grp] * acc[...], axis=0, keepdims=True), (8, GC)
-        )
-        gain_row = qe[8:9, cols(grp)]
+        gain_row = qe[GAIN_ROW : GAIN_ROW + 1, cols(grp)]
         head_of = grp * (GC // 64) + iota((GC, 128), 0) // 64
         to_dc = jnp.where(iota((GC, 128), 1) == head_of, 1.0, 0.0).astype(BF16)
         to_sx = jnp.where(iota((GC, 128), 1) == head_of + 64, 1.0, 0.0).astype(BF16)
 
         @pl.loop(0, NBLK)
-        def _(i):
-            blk = NBLK - 1 - i
+        def _(lap):
+            blk = NBLK - 1 - lap
             at = pl.ds(pl.multiple_of(blk * BLK, BLK), BLK)
-            q = q_row(blk, grp)
-            scaled = q * acc[...]
-            acc[...] = q * (scaled + ta[slot, blk])
-            sh, sl = halves(scaled)
-            ah, al = agh[slot, at, :], agl[slot, at, :]
-            b = bm[at, :]
-            gb = mm(bch[at, :], ah) + mm(bcl[at, :], ah) + mm(bch[at, :], al)
-            gb = gb + mm(b, sh) + mm(b, sl)
-            bs = mm(bsp[blk], expand[:, cols(grp)])
-            grads = (16.0 * bs) * gb + gain_row * gv[at, cols(grp)].astype(F32)
-            xo[at, cols(grp)] = grads.astype(BF16)
-            hi, lo = xh[at, cols(grp)], xl[at, cols(grp)]
+            first, second = slice(0, HALF), slice(HALF, BLK)
+            entry = acc[...]
+            acc[...] = scale(0, blk, grp) * entry + ta[slot, blk]
+            tails = jnp.sum(tf[grp, blk + 1] * entry, axis=0, keepdims=True)
+            de[pl.ds(blk, 1), cols(grp)] = tails
+            sh, sl = halves(entry)
+            b, ph, plo = bm[at, :], bch[at, :], bcl[at, :]
+            inter = mm(b, sh) + mm(b, sl)
+            a1, a2 = ags[slot, 2 * blk], ags[slot, 2 * blk + 1]
+            p2 = mm(twice(ph[:, second]), a2) + mm(plo[:, second], a2[:HALF])
+            p1 = mm(twice(ph[first, first]), a1) + mm(plo[first, first], a1[:HALF])
+            cross = scale(5, blk, grp)
+            gbs = (
+                p1 + cross * p2[first] + scale(1, blk, grp) * inter[first],
+                p2[second] + scale(2, blk, grp) * inter[second],
+            )
             sh, sl = halves(tf[grp, blk])
-            cc = cm[at, :]
-            yy = mm(cbh[at, :], hi) + mm(cbl[at, :], hi) + mm(cbh[at, :], lo)
-            yy = yy + mm(cc, sh) + mm(cc, sl)
-            sx = (hi.astype(F32) + lo.astype(F32)) * gb
-            dc = (ah.astype(F32) + al.astype(F32)) * yy - sx
-            dh, dl = halves(dc)
-            xh_, xl_ = halves(sx)
-            r = mm(dh, to_dc) + mm(dl, to_dc) + mm(xh_, to_sx) + mm(xl_, to_sx)
-            if grp == 0:
-                res[blk] = r
-            else:
-                res[blk] += r
+            cc, ph, plo = cm[at, :], cbh[at, :], cbl[at, :]
+            inter = mm(cc, sh) + mm(cc, sl)
+            x1, x2 = xs[2 * blk, :, cols(grp)], xs[2 * blk + 1, :, cols(grp)]
+            p1 = mm(twice(ph[:, first]), x1) + mm(plo[:, first], x1[:HALF])
+            p2 = mm(twice(ph[second, second]), x2) + mm(plo[second, second], x2[:HALF])
+            ys = (
+                p1[first] + scale(3, blk, grp) * inter[first],
+                p2 + cross * p1[second] + scale(4, blk, grp) * inter[second],
+            )
+            for i, (xx, aa) in enumerate(((x1, a1), (x2, a2))):
+                here = pl.ds(pl.multiple_of(blk * BLK + i * HALF, HALF), HALF)
+                part = slice(i * HALF, (i + 1) * HALF)
+                bs = mm(bsp[blk, part, :], expand[:, cols(grp)])
+                grads = bs * gbs[i] + gain_row * gv[here, cols(grp)].astype(F32)
+                xo[here, cols(grp)] = grads.astype(BF16)
+                sx = whole(xx) * gbs[i]
+                dc = whole(aa) * ys[i] - sx
+                dh, dl = halves(dc)
+                gh, gl = halves(sx)
+                r = mm(dh, to_dc) + mm(dl, to_dc) + mm(gh, to_sx) + mm(gl, to_sx)
+                if grp == 0:
+                    res[blk, part, :] = r
+                else:
+                    res[blk, part, :] += r
 
         @pl.loop(1, NHEAD)
         def _(j):
@@ -416,15 +445,13 @@
 
     head_of = iota((COLS, 128), 0) // 64
     to_dc = jnp.where(iota((COLS, 128), 1) == head_of, 1.0, 0.0).astype(F32)
-    tail = exact_mm(de[...], to_dc)
-    tail = jnp.broadcast_to(tail[0:1, :], (128, 128)).T[0:16, 0:1]
+    tails = jnp.concatenate([exact_mm(de[...], to_dc), jnp.zeros((120, 128), F32)], axis=0).T
     after = (iota((BLK, BLK), 0) >= iota((BLK, BLK), 1)).astype(F32)
-    for blk in range(NBLK - 1, -1, -1):
+    for blk in range(NBLK):
         r = res[blk].T
-        suffix = exact_mm(r[0:16], after) + tail
-        tail = suffix[:, 0:1]
+        suffix = exact_mm(r[0:16], after) + tails[0:16, blk : blk + 1]
         at = slice(blk * BLK, (blk + 1) * BLK)
-        sg_ref[:, at] = 16.0 * (r[64:80] / step_ref[:, at] - rate * suffix)
+        sg_ref[:, at] = r[64:80] / step_ref[:, at] - rate * suffix
 
     for grp in range(NG):
 
@@ -453,11 +480,9 @@
     scratch = [
         vm((LOCAL, COLS), BF16),
         vm((LOCAL, COLS), BF16),
-        vm((LOCAL, COLS), BF16),
-        vm((LOCAL, COLS), BF16),
-        vm((2, LOCAL, GC), BF16),
-        vm((2, LOCAL, GC), BF16),
-        vm((NG, NBLK, BLK, GC), F32),
+        vm((2 * NBLK, BLK, COLS), BF16),
+        vm((2, 2 * NBLK, BLK, GC), BF16),
+        vm((NG, NBLK + 1, BLK, GC), F32),
         vm((2, NBLK, BLK, GC), F32),
         vm((2, 2, CH * NGROUPS, BLK), BF16),
     ]
@@ -468,7 +493,7 @@
         vm((128, COLS), BF16),
         vm((BLK, GC), F32),
         vm((NBLK, BLK, 128), F32),
-        vm((16, COLS), F32),
+        vm((56, COLS), F32),
         vm((16, COLS), F32),
         vm((8, COLS), F32),
         vm((8, 16, 128), F32),

time: 137 us -> 135 us (0.985)
  Pallas kernels: 131 us -> 128 us
    pallas_call x1, Pallas kernels: 131 us -> 128 us  [local(): pl.pallas_call(kernel, out_shape=(jax.ShapeDtypeStruct((ROWS, NHEAD * COL...]
where the time goes in v1:
time: 135 us; the launch traced here: 134 us
  Pallas kernels  128 us (95%)
  local copies, waits for them, and re-layouts  5.27 us (4%)
    pallas_call x1, Pallas kernels, local(): pl.pallas_call(kernel, out_shape=(jax.ShapeDtypeStruct((ROWS, NHEAD * COL...  128 us
    unnamed x4, local copies, waits for them, and re-layouts  5.27 us

profile of v1, /device:TPU:4, one launch (start us, length us, event | category | flops | bytes accessed | tf_op | source)
XLA Modules:
  0.0 134.3 jit_solution(16753678643933487366)
XLA Ops:
  0.6 128.4 %shard_map.86 = (bf16[128,16384]{1,0:T(8,128)(2,1)}, f32[16,2048]{1,0:T(8,128)}) custom-call(bf16[2048,1024]{1,0:T(8,128)(2,1)} %x_hbm.1, f32[16,2048]{1,0:T(8,128)} %bitcast.8, f32[1,16]{1,0:T(1,128)} %bitcast.10, f32[1,16]{1,0:T(1,128)} %bitcast.11, bf16[16384,256]{1,0:T(8,128)(2,1)} %bitcast.6, bf16[16384,256]{1,0:T(8,128)(2,1)} %bitcast.7, ...), custom_call_target="tpu_custom_call" | custom-call | tf_op jit(solution)/shard_map/pallas_call | solution.py:517
  129.0 0.0 copy-start
  129.0 4.6 %copy.11 = bf16[128,16384]{1,0:T(8,128)(2,1)} copy(bf16[128,16384]{1,0:T(8,128)(2,1)} %get-tuple-element.8) | data formatting | bytes 8388608
  133.6 0.0 copy-done
  133.6 0.7 copy.12
Async XLA Ops:
  129.0 4.6 %copy-start = (f32[16,2048]{1,0:T(8,128)S(1)}, f32[16,2048]{1,0:T(8,128)}, u32[]{:S(2)}) copy-start(f32[16,2048]{1,0:T(8,128)} %get-tuple-element.5) | copy-start | bytes 393220

commit v2 on v1

--- a/solution.py
+++ b/solution.py
@@ -59,10 +59,10 @@
 
 def kernel(
     x_hbm, step_ref, rate_ref, gain_ref, b_hbm, c_hbm, g_hbm, out_hbm, sg_ref,
-    xo, gv, xs, ags, tf, ta, raw, bm, cm, bt, ct, cbh, cbl, bch, bcl,
+    xo, gv, xs, ags, tf, ta, raw, wide, bm, cm, bt, ct, cbh, cbl, bch, bcl,
     asp, bsp, expand, acc, res, qe, we, de, lbuf,
-    fs_tot, fs_pair, fs_chip, fs_in, as_tot, as_pair, as_chip, as_in,
-    loc_sem, raw_sem, gs, gr, os, orr, ls, lr, fps, fpr, fys, fyr, aps, apr, ays, ayr,
+    fs_tot, fs_pair, fs_chip, fs_in, fs_half, as_tot, as_pair, as_chip, as_in, as_half,
+    loc_sem, raw_sem, gs, gr, os, orr, ls, lr, fps, fpr, fys, fyr, fhs, fhr, aps, apr, ays, ayr, ahs, ahr,
 ):
     c = lax.axis_index("ctx")
     h = lax.axis_index("head")
@@ -117,12 +117,13 @@
             device_id_type=MESH,
         )
 
-    for grp in range(NG):
-
+    def send_grad(grp):
         @pl.loop(1, NHEAD)
         def _(j):
             grad_in(grp, j).start()
 
+    send_grad(0)
+    send_grad(1)
     own_g = pltpu.make_async_copy(
         g_hbm.at[:, pl.ds(pl.multiple_of(h * COLS, COLS), COLS)],
         gv.at[pl.ds(pl.multiple_of(h * ROWS, ROWS), ROWS)],
@@ -166,9 +167,6 @@
     def _(j):
         log_send(j).start()
 
-    pick = jnp.where(iota((32, 256), 1) == iota((32, 256), 0) * NGROUPS + group, 1.0, 0.0)
-    pick = pick.astype(BF16)
-
     @pl.loop(0, NCH)
     def _(i):
         @pl.when(i + 1 < NCH)
@@ -181,9 +179,11 @@
         slot = lax.rem(i, 2)
         at = pl.multiple_of(i * CH, CH)
         for which, target in ((0, bm), (1, cm)):
-            for part in range(CH // 32):
-                rows = raw[slot, which, pl.ds(part * 256, 256), :]
-                target[pl.ds(at + part * 32, 32), :] = mm(pick, rows).astype(BF16)
+            for n in range(2):
+                lanes = slice(n * 128, n * 128 + 128)
+                wide[which, n] = raw[slot, which, :, lanes].astype(F32)
+                rows = wide[which, n, pl.ds(group, CH, stride=NGROUPS), :]
+                target[pl.ds(at, CH), lanes] = rows.astype(BF16)
 
     low = iota((BLK, BLK), 0) >= iota((BLK, BLK), 1)
 
@@ -209,6 +209,14 @@
             src.at[grp], dst.at[dy - 1, grp], s.at[dy - 1, grp], r.at[dy - 1, grp],
             device_id=(lax.rem(to, 4) * 2 + k, h), device_id_type=MESH,
         )
+
+    def half_copy(ref, s, r, grp):
+        return pltpu.make_async_remote_copy(
+            ref.at[grp, k], ref.at[grp, k], s.at[grp], r.at[grp],
+            device_id=(y * 2 + 1 - k, h), device_id_type=MESH,
+        )
+
+    my_half = pl.ds(pl.multiple_of(k * HALF, HALF), HALF)
 
     def scale(which, blk, grp):
         return qe[pl.ds(which * NBLK + blk, 1), cols(grp)]
@@ -236,7 +244,8 @@
     def forward_chip(grp):
         pair_copy(fs_tot, fs_pair, fps, fpr, grp).wait()
         fs_chip[grp] = (
-            we[0:1, cols(grp)] * fs_tot[grp] + we[1:2, cols(grp)] * fs_pair[grp]
+            we[0:1, cols(grp)] * fs_tot[grp, my_half, :]
+            + we[1:2, cols(grp)] * fs_pair[grp, my_half, :]
         ).astype(BF16)
         for dy in (1, 2, 3):
 
@@ -244,16 +253,21 @@
             def _():
                 line_copy(fs_chip, fs_in, fys, fyr, grp, dy, True).start()
 
-    def forward_states(grp):
-        acc[...] = jnp.zeros_like(acc)
+    def forward_half(grp):
+        fs_half[grp, k] = jnp.zeros((HALF, GC), F32)
         for dy in (1, 2, 3):
 
             @pl.when(y - dy >= 0)
             def _():
                 line_copy(fs_chip, fs_in, fys, fyr, grp, dy, True).wait_recv()
-                acc[...] += we[2 + dy : 3 + dy, cols(grp)] * fs_in[dy - 1, grp].astype(F32)
-
-        acc[...] = we[2:3, cols(grp)] * acc[...]
+                fs_half[grp, k] += we[2 + dy : 3 + dy, cols(grp)] * fs_in[dy - 1, grp].astype(F32)
+
+        half_copy(fs_half, fhs, fhr, grp).start()
+
+    def forward_states(grp):
+        half_copy(fs_half, fhs, fhr, grp).wait()
+        acc[0:HALF, :] = we[2:3, cols(grp)] * fs_half[grp, 0]
+        acc[HALF:BLK, :] = we[2:3, cols(grp)] * fs_half[grp, 1]
 
         @pl.when(k == 1)
         def _():
@@ -296,12 +310,26 @@
 
     def adjoint_chip(grp):
         pair_copy(as_tot, as_pair, aps, apr, grp).wait()
-        as_chip[grp] = we[6:7, cols(grp)] * as_tot[grp] + we[7:8, cols(grp)] * as_pair[grp]
+        as_chip[grp] = (
+            we[6:7, cols(grp)] * as_tot[grp, my_half, :]
+            + we[7:8, cols(grp)] * as_pair[grp, my_half, :]
+        )
         for dy in (1, 2, 3):
 
             @pl.when(y - dy >= 0)
             def _():
                 line_copy(as_chip, as_in, ays, ayr, grp, dy, False).start()
+
+    def adjoint_half(grp):
+        as_half[grp, k] = jnp.zeros((HALF, GC), F32)
+        for dy in (1, 2, 3):
+
+            @pl.when(y + dy < NY)
+            def _():
+                line_copy(as_chip, as_in, ays, ayr, grp, dy, False).wait_recv()
+                as_half[grp, k] += we[8 + dy : 9 + dy, cols(grp)] * as_in[dy - 1, grp]
+
+        half_copy(as_half, ahs, ahr, grp).start()
 
     def grad_out(grp, j):
         to = head_at(j)
@@ -323,15 +351,9 @@
 
     def finish(grp):
         slot = grp % 2
-        acc[...] = jnp.zeros_like(acc)
-        for dy in (1, 2, 3):
-
-            @pl.when(y + dy < NY)
-            def _():
-                line_copy(as_chip, as_in, ays, ayr, grp, dy, False).wait_recv()
-                acc[...] += we[8 + dy : 9 + dy, cols(grp)] * as_in[dy - 1, grp]
-
-        acc[...] = we[8:9, cols(grp)] * acc[...]
+        half_copy(as_half, ahs, ahr, grp).wait()
+        acc[0:HALF, :] = we[8:9, cols(grp)] * as_half[grp, 0]
+        acc[HALF:BLK, :] = we[8:9, cols(grp)] * as_half[grp, 1]
 
         @pl.when(core0)
         def _():
@@ -394,10 +416,6 @@
 
         own_out(grp).start()
 
-    x_copy.wait()
-    for grp in range(NG):
-        forward_local(grp)
-
     @pl.loop(1, 8)
     def _(j):
         log_send(j).wait()
@@ -422,26 +440,34 @@
     logs = put(logs, 10, log_chip(y + 1))
     logs = put(logs, 11, log_chip(y + 1) + log_chip(y + 2))
     we[...] = mm(pack3(jnp.exp(logs))[:16], expand[...])
+    x_copy.wait()
     own_g.wait()
 
-    for grp in range(NG):
-        forward_chip(grp)
+    send_grad(2)
     adjoint_local(0)
+    send_grad(3)
+    forward_local(0)
     adjoint_chip(0)
+    forward_chip(0)
+    forward_local(1)
+    adjoint_half(0)
+    forward_half(0)
+    forward_chip(1)
+    adjoint_local(1)
     forward_states(0)
-    adjoint_local(1)
-    adjoint_chip(1)
-    forward_states(1)
     finish(0)
-    adjoint_local(2)
-    adjoint_chip(2)
-    forward_states(2)
-    finish(1)
-    adjoint_local(3)
-    adjoint_chip(3)
-    forward_states(3)
-    finish(2)
-    finish(3)
+    for grp in range(1, NG):
+        adjoint_chip(grp)
+        if grp + 1 < NG:
+            forward_local(grp + 1)
+        forward_half(grp)
+        if grp + 1 < NG:
+            forward_chip(grp + 1)
+        adjoint_half(grp)
+        if grp + 1 < NG:
+            adjoint_local(grp + 1)
+        forward_states(grp)
+        finish(grp)
 
     head_of = iota((COLS, 128), 0) // 64
     to_dc = jnp.where(iota((COLS, 128), 1) == head_of, 1.0, 0.0).astype(F32)
@@ -476,6 +502,7 @@
     vm = pltpu.VMEM
     dma = pltpu.SemaphoreType.DMA
     state = (NG, BLK, GC)
+    half = (NG, HALF, GC)
     proj = vm((LOCAL, BLK), BF16)
     scratch = [
         vm((LOCAL, COLS), BF16),
@@ -486,6 +513,7 @@
         vm((2, NBLK, BLK, GC), F32),
         vm((2, 2, CH * NGROUPS, BLK), BF16),
     ]
+    scratch += [vm((2, 2, CH * NGROUPS, 128), F32)]
     scratch += [proj] * 8
     scratch += [
         vm((NBLK, BLK, 128), BF16),
@@ -499,18 +527,20 @@
         vm((8, 16, 128), F32),
         vm(state, F32),
         vm(state, F32),
-        vm(state, BF16),
-        vm((3,) + state, BF16),
+        vm(half, BF16),
+        vm((3,) + half, BF16),
+        vm((NG, 2, HALF, GC), F32),
         vm(state, F32),
         vm(state, F32),
-        vm(state, F32),
-        vm((3,) + state, F32),
+        vm(half, F32),
+        vm((3,) + half, F32),
+        vm((NG, 2, HALF, GC), F32),
         dma((2 + NG,)),
         dma((2, 2)),
         dma((NG, NHEAD)), dma((NG, NHEAD)), dma((NG, NHEAD)), dma((NG, NHEAD)),
         dma((8,)), dma((8,)),
-        dma((NG,)), dma((NG,)), dma((3, NG)), dma((3, NG)),
-        dma((NG,)), dma((NG,)), dma((3, NG)), dma((3, NG)),
+        dma((NG,)), dma((NG,)), dma((3, NG)), dma((3, NG)), dma((NG,)), dma((NG,)),
+        dma((NG,)), dma((NG,)), dma((3, NG)), dma((3, NG)), dma((NG,)), dma((NG,)),
     ]
     hbm = pl.BlockSpec(memory_space=pl.ANY)
     vmem = pl.BlockSpec(memory_space=pltpu.VMEM)

time: 135 us -> 122 us (0.904)
  Pallas kernels: 128 us -> 115 us
    pallas_call x1, Pallas kernels: 128 us -> 115 us  [local(): pl.pallas_call(kernel, out_shape=(jax.ShapeDtypeStruct((ROWS, NHEAD * COL...]
where the time goes in v2:
time: 122 us; the launch traced here: 120 us
  Pallas kernels  115 us (94%)
  local copies, waits for them, and re-layouts  5.27 us (4%)
    pallas_call x1, Pallas kernels, local(): pl.pallas_call(kernel, out_shape=(jax.ShapeDtypeStruct((ROWS, NHEAD * COL...  115 us
    unnamed x4, local copies, waits for them, and re-layouts  5.27 us

profile of v2, /device:TPU:4, one launch (start us, length us, event | category | flops | bytes accessed | tf_op | source)
XLA Modules:
  0.0 120.4 jit_solution(7091579970634858087)
XLA Ops:
  0.6 114.5 %shard_map.86 = (bf16[128,16384]{1,0:T(8,128)(2,1)}, f32[16,2048]{1,0:T(8,128)}) custom-call(bf16[2048,1024]{1,0:T(8,128)(2,1)} %x_hbm.1, f32[16,2048]{1,0:T(8,128)} %bitcast.8, f32[1,16]{1,0:T(1,128)} %bitcast.10, f32[1,16]{1,0:T(1,128)} %bitcast.11, bf16[16384,256]{1,0:T(8,128)(2,1)} %bitcast.6, bf16[16384,256]{1,0:T(8,128)(2,1)} %bitcast.7, ...), custom_call_target="tpu_custom_call" | custom-call | tf_op jit(solution)/shard_map/pallas_call | solution.py:547
  115.2 0.0 copy-start
  115.2 4.6 %copy.11 = bf16[128,16384]{1,0:T(8,128)(2,1)} copy(bf16[128,16384]{1,0:T(8,128)(2,1)} %get-tuple-element.8) | data formatting | bytes 8388608
  119.8 0.0 copy-done
  119.8 0.7 copy.12
Async XLA Ops:
  115.2 4.6 %copy-start = (f32[16,2048]{1,0:T(8,128)S(1)}, f32[16,2048]{1,0:T(8,128)}, u32[]{:S(2)}) copy-start(f32[16,2048]{1,0:T(8,128)} %get-tuple-element.5) | copy-start | bytes 393220

commit v3 on v2

--- a/solution.py
+++ b/solution.py
@@ -20,6 +20,7 @@
 CH = 128
 NCH = LOCAL // CH
 MESH = pl.DeviceIdType.MESH
+ORDER = (10, 5, 15, 7, 13, 6, 14, 9, 11, 2, 8, 1, 3, 4, 12)
 F32 = jnp.float32
 BF16 = jnp.bfloat16
 
@@ -72,10 +73,10 @@
     core0 = k == 0
 
     def head_at(j):
-        return lax.rem(hx + j // 4, 4) * 4 + lax.rem(hz + lax.rem(j, 4), 4)
+        return lax.rem(hx + j // 4, 4) * 4 + lax.rem(hz + (j - (j // 4) * 4), 4)
 
     def head_from(j):
-        return lax.rem(hx + 4 - j // 4, 4) * 4 + lax.rem(hz + 4 - lax.rem(j, 4), 4)
+        return lax.rem(hx + 4 - j // 4, 4) * 4 + lax.rem(hz + 4 - (j - (j // 4) * 4), 4)
 
     def cols(grp):
         return pl.ds(grp * GC, GC)
@@ -118,8 +119,7 @@
         )
 
     def send_grad(grp):
-        @pl.loop(1, NHEAD)
-        def _(j):
+        for j in ORDER:
             grad_in(grp, j).start()
 
     send_grad(0)
@@ -384,9 +384,8 @@
                 p1 + cross * p2[first] + scale(1, blk, grp) * inter[first],
                 p2[second] + scale(2, blk, grp) * inter[second],
             )
-            sh, sl = halves(tf[grp, blk])
             cc, ph, plo = cm[at, :], cbh[at, :], cbl[at, :]
-            inter = mm(cc, sh) + mm(cc, sl)
+            inter = mm(cc, tf[grp, blk].astype(BF16))
             x1, x2 = xs[2 * blk, :, cols(grp)], xs[2 * blk + 1, :, cols(grp)]
             p1 = mm(twice(ph[:, first]), x1) + mm(plo[:, first], x1[:HALF])
             p2 = mm(twice(ph[second, second]), x2) + mm(plo[second, second], x2[:HALF])
@@ -410,8 +409,7 @@
                 else:
                     res[blk, part, :] += r
 
-        @pl.loop(1, NHEAD)
-        def _(j):
+        for j in ORDER:
             grad_out(grp, j).start()
 
         own_out(grp).start()

time: 122 us -> 121 us (level)
  no operation moved by 1% of the time
where the time goes in v3:
time: 121 us; the launch traced here: 120 us
  Pallas kernels  114 us (94%)
  local copies, waits for them, and re-layouts  5.27 us (4%)
    pallas_call x1, Pallas kernels, local(): pl.pallas_call(kernel, out_shape=(jax.ShapeDtypeStruct((ROWS, NHEAD * COL...  114 us
    unnamed x4, local copies, waits for them, and re-layouts  5.27 us

profile of v3, /device:TPU:4, one launch (start us, length us, event | category | flops | bytes accessed | tf_op | source)
XLA Modules:
  0.0 119.8 jit_solution(13844818762774393830)
XLA Ops:
  0.6 113.8 %shard_map.86 = (bf16[128,16384]{1,0:T(8,128)(2,1)}, f32[16,2048]{1,0:T(8,128)}) custom-call(bf16[2048,1024]{1,0:T(8,128)(2,1)} %x_hbm.1, f32[16,2048]{1,0:T(8,128)} %bitcast.8, f32[1,16]{1,0:T(1,128)} %bitcast.10, f32[1,16]{1,0:T(1,128)} %bitcast.11, bf16[16384,256]{1,0:T(8,128)(2,1)} %bitcast.6, bf16[16384,256]{1,0:T(8,128)(2,1)} %bitcast.7, ...), custom_call_target="tpu_custom_call" | custom-call | tf_op jit(solution)/shard_map/pallas_call | solution.py:545
  114.5 0.0 copy-start
  114.5 4.6 %copy.11 = bf16[128,16384]{1,0:T(8,128)(2,1)} copy(bf16[128,16384]{1,0:T(8,128)(2,1)} %get-tuple-element.8) | data formatting | bytes 8388608
  119.1 0.0 copy-done
  119.1 0.7 copy.12
Async XLA Ops:
  114.5 4.6 %copy-start = (f32[16,2048]{1,0:T(8,128)S(1)}, f32[16,2048]{1,0:T(8,128)}, u32[]{:S(2)}) copy-start(f32[16,2048]{1,0:T(8,128)} %get-tuple-element.5) | copy-start | bytes 393220
